TPU v7x, 512 devices: a whole 4x4x16 slice. The times are simulated.
512 devices in a mesh: ctx: 16 (over z_lo, core), head: 32 (over z_hi, y, x).
Axes of the slice: x: 4, y: 4, z: 16 (z_hi: 2, z_lo: 8; z = z_hi * 8 + z_lo), core: 2. Of those that a mesh axis runs over, the one named last changes fastest.
Arguments:
- queries: bfloat16 [4096, 8192], P('ctx', 'head'), may hold values from -5 to 5
- key_rows: bfloat16 [4096, 1024], P('ctx'), may hold values from -5 to 5
- value_rows: bfloat16 [4096, 1024], P('ctx'), may hold values from -6 to 6
- state_input: bfloat16 [4096, 8192], P('ctx', 'head'), may hold values from -6 to 6
- state_write: bfloat16 [4096, 8192], P('ctx', 'head'), may hold values from -0.119628906 to 0.119628906
- state_read: bfloat16 [4096, 8192], P('ctx', 'head'), may hold values from -6 to 6
- gate_input: bfloat16 [4096, 8192], P('ctx', 'head'), may hold values from -6 to 6
- decay_codes: int32 [4096, 64], P('ctx', 'head'), may hold values from 1 to 8192
- decay_rates: float32 [64], P('head'), may hold values from 2.9296875e-05 to 0.03
- skip_gain: float32 [64], P('head'), may hold values from 0.5 to 2
- norm_gain: float32 [8192], P('head'), may hold values from 0.5 to 1.5
- attend_readout: float32 [8192], P('head'), may hold values from -1.5 to 1.5
- state_readout: float32 [8192], P('head'), may hold values from -0.12 to 0.12
- segment_index: int32 [4096], P('ctx'), may hold values from 0 to 31, never falling along the last dimension, each value on 1 to 256 neighbouring positions
Outputs:
- attended: bfloat16 [4096, 8192], P('ctx', 'head')
- state_mixed: bfloat16 [4096, 8192], P('ctx', 'head')
- segment_values: float32 [32], replicated
All inputs are finite; a program needn't handle non-finite values.
Results may differ from a plain program's by a relative error of at most 0.018.
Values may be sent and summed in bfloat16 or wider, within the bound.
No kernel may reach another device: no remote copies, remote signals or barrier semaphores. Data moves between devices by JAX's collectives and lax.ppermute only.
A program may use at most 64 MiB of HBM per device.

v0:
```python
import math
import jax
import jax.numpy as jnp
from jax import lax
from jax.sharding import PartitionSpec as P

HEADS = 64
KV_HEADS = 8
HEAD_DIM = 128
SCAN_HEADS = 64
SCAN_DIM = 128
STATE = 128
BLOCK = 128
SEG_MEAN = 128
floor_score = -1e30


def prefix(array, axis, combine, identity):
    count, index = (lax.axis_size(axis), lax.axis_index(axis))
    everything = jax.tree.map(
        lambda part, kind: lax.all_gather(part.astype(kind), axis),
        array,
        (jnp.bfloat16, jnp.bfloat16),
    )
    start = jax.tree.map(
        lambda part, zero: jnp.broadcast_to(jnp.asarray(zero, part.dtype), part.shape),
        array,
        identity,
    )

    def turn(k, before):
        reached = k < index
        new = combine(
            before, jax.tree.map(lambda part, own: part[k].astype(own.dtype), everything, array)
        )
        return jax.tree.map(lambda a, b: jnp.where(reached, a, b), new, before)

    return lax.fori_loop(0, count, turn, start)


def absorb_group(inner, keys_piece, values_piece, start, third_request_vector, query_pos):
    rows = keys_piece.shape[0]
    per_head_dimension = third_request_vector.shape[2]
    width = math.gcd(rows, 512)
    scale = per_head_dimension ** (-0.5)

    def one_block(index, state):
        top, total, summed = state
        begin = index * width
        key_block = lax.dynamic_slice_in_dim(keys_piece, begin, width, 0)
        value_block = lax.dynamic_slice_in_dim(values_piece, begin, width, 0)
        scores = (
            jnp.einsum(
                "qhd,kd->qhk", third_request_vector, key_block, preferred_element_type=jnp.float32
            )
            * scale
        )
        key_pos = begin + jnp.arange(width, dtype=jnp.int32)
        allowed = (key_pos[None, :] <= query_pos[:, None])[:, None, :]
        masked = jnp.where(allowed, scores, floor_score)
        new_top = jnp.maximum(top, jnp.max(masked, axis=2))
        weights = jnp.where(allowed, jnp.exp(masked - new_top[:, :, None]), 0.0)
        fade = jnp.exp(top - new_top)
        total = total * fade + jnp.sum(weights, axis=2)
        summed = summed * fade[:, :, None] + jnp.einsum(
            "qhk,kd->qhd",
            weights.astype(jnp.bfloat16),
            value_block,
            preferred_element_type=jnp.float32,
        )
        return (new_top, total, summed)

    def compute(state):
        return lax.fori_loop(0, rows // width, one_block, state)

    def keep(state):
        return state

    needed = jnp.logical_and(start >= 0, start <= jnp.max(query_pos))
    return lax.cond(needed, compute, keep, inner)


def merge_state_pairs(earlier, later):
    return (earlier[0] * later[0], later[0][:, None, None] * earlier[1] + later[1])


def per_device(
    queries,
    key_rows,
    value_rows,
    state_input,
    state_write,
    state_read,
    gate_input,
    decay_codes,
    decay_rates,
    skip_gain,
    norm_gain,
    attend_readout,
    state_readout,
    segment_index,
):
    tokens_here = queries.shape[0]
    heads_here = queries.shape[1] // HEAD_DIM
    n_ctx = lax.axis_size("ctx")
    position = lax.axis_index("ctx")
    first = position * tokens_here
    shared_head = lax.axis_index("head") * heads_here // (HEADS // KV_HEADS)
    key_mine = lax.dynamic_slice_in_dim(key_rows, shared_head * HEAD_DIM, HEAD_DIM, 1)
    value_mine = lax.dynamic_slice_in_dim(value_rows, shared_head * HEAD_DIM, HEAD_DIM, 1)
    scan_here = decay_rates.shape[0]
    blocks = tokens_here // BLOCK
    inputs_four = state_input.reshape(blocks, BLOCK, scan_here, SCAN_DIM)
    write_four = state_write.reshape(blocks, BLOCK, scan_here, STATE)
    read_four = state_read.reshape(blocks, BLOCK, scan_here, STATE)
    log_decay = -decay_rates[None, :] * decay_codes.astype(jnp.float32)
    run = jnp.cumsum(log_decay.reshape(blocks, BLOCK, scan_here), axis=1)
    run_heads = jnp.transpose(run, (0, 2, 1))
    gap = run_heads[:, :, :, None] - run_heads[:, :, None, :]
    places = jnp.arange(BLOCK, dtype=jnp.int32)
    lower = places[:, None] >= places[None, :]
    decay = jnp.where(lower[None, None], jnp.exp(jnp.minimum(gap, 0.0)), 0.0)
    scan_scores = jnp.einsum(
        "bthn,bshn->bhts", read_four, write_four, preferred_element_type=jnp.float32
    )
    mix = (scan_scores * decay).astype(jnp.bfloat16)
    local = jnp.einsum("bhts,bshp->bthp", mix, inputs_four, preferred_element_type=jnp.float32)
    tail = jnp.exp(run[:, -1:, :] - run)
    written = (write_four.astype(jnp.float32) * tail[:, :, :, None]).astype(jnp.bfloat16)
    block_state = jnp.einsum(
        "bshn,bshp->bhnp", written, inputs_four, preferred_element_type=jnp.float32
    )
    block_fade = jnp.exp(run[:, -1, :])

    def carry_step(state, item):
        current, product = state
        fade_now, new_state = item
        return (
            (fade_now[:, None, None] * current + new_state, product * fade_now),
            (current, product),
        )

    start_state = (
        jnp.zeros((scan_here, STATE, SCAN_DIM), jnp.float32),
        jnp.ones((scan_here,), jnp.float32),
    )
    (end_state, total_fade), (entering_local, fade_before) = lax.scan(
        carry_step, start_state, (block_fade, block_state)
    )
    prefix_pair = prefix(
        (total_fade, end_state),
        "ctx",
        merge_state_pairs,
        (jnp.ones_like(total_fade), jnp.zeros_like(end_state)),
    )
    incoming = prefix_pair[1]
    entering = entering_local + fade_before[:, :, None, None] * incoming[None]
    carried = jnp.exp(run)[:, :, :, None] * jnp.einsum(
        "bthn,bhnp->bthp", read_four.astype(jnp.float32), entering, precision=lax.Precision.HIGHEST
    )
    mixed_y = local + carried + skip_gain[None, None, :, None] * inputs_four.astype(jnp.float32)
    gated = mixed_y.reshape(tokens_here, scan_here * SCAN_DIM) * jax.nn.silu(
        gate_input.astype(jnp.float32)
    )
    squares = lax.psum(jnp.sum(gated * gated, axis=1), "head")
    state_mixed = (
        gated * lax.rsqrt(squares / (SCAN_HEADS * SCAN_DIM) + 1e-05)[:, None] * norm_gain[None, :]
    ).astype(jnp.bfloat16)
    groups = (
        (
            queries.reshape(tokens_here, heads_here, HEAD_DIM),
            first + jnp.arange(tokens_here, dtype=jnp.int32),
        ),
    )
    initial = tuple(
        (
            (
                jnp.full((item[0].shape[0], heads_here), floor_score, jnp.float32),
                jnp.zeros((item[0].shape[0], heads_here), jnp.float32),
                jnp.zeros((item[0].shape[0], heads_here, HEAD_DIM), jnp.float32),
            )
            for item in groups
        )
    )
    pieces = (
        lax.all_gather(key_mine, "ctx", axis=0, tiled=True),
        lax.all_gather(value_mine, "ctx", axis=0, tiled=True),
    )
    start = jnp.int32(0)
    inner = tuple(
        (
            absorb_group(
                initial[number], pieces[0], pieces[1], start, groups[number][0], groups[number][1]
            )
            for number in range(len(groups))
        )
    )
    outputs = []
    for state in inner:
        top, total, summed = state
        outputs.append(
            (summed / total[:, :, None])
            .reshape(summed.shape[0], heads_here * HEAD_DIM)
            .astype(jnp.bfloat16)
        )
    attended = outputs[0]
    score = jnp.sum(attended.astype(jnp.float32) * attend_readout[None, :], axis=1)
    score = score + jnp.sum(state_mixed.astype(jnp.float32) * state_readout[None, :], axis=1)
    segment_count = tokens_here * n_ctx // SEG_MEAN
    member = (segment_index[:, None] == jnp.arange(segment_count, dtype=jnp.int32)[None, :]).astype(
        jnp.float32
    )
    partial_sums = jnp.dot(score, member, precision=lax.Precision.HIGHEST)
    counted = jnp.sum(member, axis=0) * (lax.axis_index("head") == 0).astype(jnp.float32)
    sums, counts = lax.psum((partial_sums, counted), ("ctx", "head"))
    return (attended, state_mixed, sums / counts)


def solution(mesh):
    in_specs = (
        P("ctx", "head"),
        P("ctx", None),
        P("ctx", None),
        P("ctx", "head"),
        P("ctx", "head"),
        P("ctx", "head"),
        P("ctx", "head"),
        P("ctx", "head"),
        P("head"),
        P("head"),
        P("head"),
        P("head"),
        P("head"),
        P("ctx"),
    )
    out_specs = (P("ctx", "head"), P("ctx", "head"), P())
    return jax.shard_map(
        per_device, mesh=mesh, in_specs=in_specs, out_specs=out_specs, check_vma=False
    )
```

profile of v0, /device:TPU:1, one launch (start us, length us, event | category | flops | bytes accessed | tf_op | source)
XLA Modules:
  0.0 475.2 jit_solution(627773776391355571)
XLA Ops:
  7.3 0.7 copy-done.12
  8.5 0.8 copy-done.2
  9.5 0.8 copy-done.3
  10.9 0.6 convert_element_type.90
  11.7 0.7 constant_dynamic-slice_fusion.2
  12.4 1.5 constant_dynamic-slice_fusion.1
  13.9 0.7 fusion.49
  15.5 1.3 dynamic-slice
  17.6 51.5 %all-reduce = bf16[32]{0:T(256)(128)(2,1)S(1)} all-reduce(bf16[32]{0:T(256)(128)(2,1)S(1)} %dynamic-update-slice), channel_id=2, replica_groups=mesh['ctx'=16,'head'=32] {'ctx'}, use_global_device_ids=true, to_apply=%add | all-reduce | flops 32 | bytes 128
  69.2 0.6 copy-done.11
  70.3 45.0 %all-gather.10.cloned.1.call-done = bf16[32,128,128]{2,1,0:T(8,128)(2,1)} async-done(((bf16[2,128,128]{2,1,0:T(8,128)(2,1)}), bf16[32,128,128]{2,1,0:T(8,128)(2,1)}) %all-gather.10.cloned.1.call-update) | async-done | bytes 1048592 | tf_op jit(solution)/shard_map/all_gather | solution.py:21
  115.3 15.6 %while.53 = (s32[]{:T(128)}, f32[2,128,128]{2,1,0:T(8,128)S(1)}, s32[]{:T(128)}, bf16[16,2]{1,0:T(8,128)(2,1)S(1)}, bf16[16,2,128,128]{3,2,1,0:T(8,128)(2,1)}) while((s32[]{:T(128)}, f32[2,128,128]{2,1,0:T(8,128)S(1)}, s32[]{:T(128)}, bf16[16,2]{1,0:T(8,128)(2,1)S(1)}, bf16[16,2,128,128]{3,2,1,0:T(8,128)(2,1)}) %tuple.138), condition=%wide.region_11.12_spmd.clone.clone, body=%wide.region_10.11_spmd.clone.sunk.clone | while | flops 163846 | bytes 327797 | solution.py:38
  115.3 0.9 fusion.84
  116.3 0.9 fusion.84
  117.3 0.9 fusion.84
  118.3 0.9 fusion.84
  119.2 0.9 fusion.84
  120.2 0.9 fusion.84
  121.2 0.9 fusion.84
  122.2 0.9 fusion.84
  123.1 0.9 fusion.84
  124.1 0.9 fusion.84
  125.1 0.9 fusion.84
  126.1 0.9 fusion.84
  127.0 0.9 fusion.84
  128.0 0.9 fusion.84
  129.0 0.9 fusion.84
  130.0 0.9 fusion.84
  130.9 0.6 copy-done.10
  132.2 0.7 copy-done.1
  133.1 141.2 %psum.21 = f32[256]{0:T(256)S(1)} all-reduce(f32[256]{0:T(256)S(1)} %multiply_reduce_fusion.2), channel_id=1, replica_groups=mesh['ctx'=16,'head'=32] {'head'}, use_global_device_ids=true, to_apply=%region_13.14 | all-reduce | flops 256 | bytes 2048 | tf_op jit(solution)/shard_map/psum | solution.py:165
  274.2 45.6 %all-gather.8.cloned.1.call-done = bf16[4096,128]{1,0:T(8,128)(2,1)} async-done(((bf16[256,128]{1,0:T(8,128)(2,1)}), bf16[4096,128]{1,0:T(8,128)(2,1)}) %all-gather.8.cloned.1.call-update) | async-done | bytes 1048592 | tf_op jit(solution)/shard_map/all_gather | solution.py:187
  319.9 40.2 %conditional.1 = (f32[256,2]{0,1:T(2,128)}, f32[256,2,128]{2,0,1:T(8,128)}) conditional(s32[]{:T(128)} %convert_element_type.82, () %tuple.48, (bf16[256,256]{1,0:T(8,128)(2,1)S(1)}, s32[256]{0:T(256)S(1)}, bf16[4096,128]{1,0:T(8,128)(2,1)}, bf16[4096,128]{1,0:T(8,128)(2,1)}) %tuple.137), branch_computations={%region_1.2_spmd, %region_2.7_spmd} | conditional | flops 136907776 | bytes 5149947 | solution.py:80
  320.1 40.0 %while.51 = (s32[]{:T(128)}, f32[256,2]{0,1:T(2,128)S(1)}, f32[256,2]{0,1:T(2,128)}, f32[256,2,128]{2,0,1:T(8,128)}, s32[256]{0:T(256)S(1)}, /*index=5*/bf16[409...) while((s32[]{:T(128)}, f32[256,2]{0,1:T(2,128)S(1)}, ...), condition=%wide.region_6.6_spmd.clone.clone, body=%wide.region_3.5_spmd.clone.sunk.clone | while | flops 136907776 | bytes 4625571 | solution.py:74
  320.3 1.2 fusion.79
  321.8 0.6 fusion.82
  322.4 2.1 convolution_add_fusion.3
  324.6 1.2 fusion.79
  326.1 1.3 fusion.82
  327.3 2.2 convolution_add_fusion.3
  329.7 1.2 fusion.79
  331.1 1.3 fusion.82
  332.4 2.2 convolution_add_fusion.3
  334.8 1.2 fusion.79
  336.2 1.3 fusion.82
  337.5 2.2 convolution_add_fusion.3
  339.9 1.2 fusion.79
  341.3 1.3 fusion.82
  342.6 2.2 convolution_add_fusion.3
  345.0 1.2 fusion.79
  346.4 1.3 fusion.82
  347.7 2.2 convolution_add_fusion.3
  350.1 1.2 fusion.79
  351.5 1.3 fusion.82
  352.8 2.2 convolution_add_fusion.3
  355.1 1.2 fusion.79
  356.6 1.3 fusion.82
  357.9 2.2 convolution_add_fusion.3
  360.1 0.7 copy-done.7
  360.8 1.2 multiply_reduce_fusion.1
  362.0 0.8 multiply_reduce_fusion
  362.9 0.7 copy_bitcast_fusion
  363.6 104.5 %all-reduce.1 = (f32[32]{0:T(128)S(1)}, f32[32]{0:T(128)S(1)}) all-reduce(f32[32]{0:T(128)S(1)} %convolution_bitcast_fusion.2, f32[32]{0:T(128)S(1)} %broadcast_multiply_fusion), channel_id=1, replica_groups=mesh['ctx'=16,'head'=32] {'ctx','head'}, use_global_device_ids=true, to_apply=%region_16.17 | all-reduce | flops 64 | bytes 512 | tf_op jit(solution)/shard_map/psum | solution.py:215
  468.1 0.5 div.37
  (131 shorter events, 7.2 us)
Async XLA Ops:
  7.2 4.5 copy-start
  7.2 108.1 %all-gather.10.cloned.1.call-start = ((), (), s32[]{:S(2)}) async-start(), calls=%async_computation.2 | async-start | bytes 1114112 | tf_op jit(solution)/shard_map/all_gather | solution.py:21
  7.2 0.7 copy-start.12
  7.3 0.7 copy-start.6
  8.4 0.9 copy-start.2
  9.4 0.9 copy-start.3
  11.6 262.6 %all-gather.6.cloned.1.call-start = ((), (), s32[]{:S(2)}) async-start(), calls=%async_computation | async-start | bytes 1114112 | tf_op jit(solution)/shard_map/all_gather | solution.py:186
  12.3 307.5 %all-gather.8.cloned.1.call-start = ((), (), s32[]{:S(2)}) async-start(), calls=%async_computation.1 | async-start | bytes 1114112 | tf_op jit(solution)/shard_map/all_gather | solution.py:187
  13.9 1.5 copy-start.4
  69.2 0.7 copy-start.11
  130.9 0.7 copy-start.10
  132.0 0.9 copy-start.1
  132.9 187.0 %copy-start.5 = (bf16[256,256]{1,0:T(8,128)(2,1)S(1)}, bf16[256,256]{1,0:T(8,128)(2,1)}, u32[]{:S(2)}) copy-start(bf16[256,256]{1,0:T(8,128)(2,1)} %param.22) | copy-start | bytes 393220
  360.1 0.7 copy-start.7
  360.8 1.2 copy-start.8
  360.8 1.2 copy-start.9
Sparse Core Ops, SparseCore 0:
  11.7 103.5 all-gather.9
  118.0 99.8 all-gather.5
  220.6 99.2 all-gather.7
where the time goes:
time: 477 us; the launch traced here: 475 us
  blocking collectives  297 us (62%)
  waiting for transfers between devices  90.7 us (19%)
  other arithmetic  32.4 us (7%)
  matrix products  28.1 us (6%)
  between operations  15.3 us (3%)
  local copies, waits for them, and re-layouts  10.5 us (2%)
    psum x1, blocking collectives, per_device(): squares = lax.psum(jnp.sum(gated * gated, axis=1), 'head')  141 us
    psum x1, blocking collectives, per_device(): sums, counts = lax.psum((partial_sums, counted), ('ctx', 'head'))  105 us
    unnamed x1, blocking collectives  51.5 us
    all_gather x1, waiting for transfers between devices, per_device(): lax.all_gather(value_mine, 'ctx', axis=0, tiled=True)  45.6 us
    all_gather x1, waiting for transfers between devices, prefix(): lax.all_gather(part.astype(kind), axis)  45 us
    dot_general x8, matrix products, one_block(): jnp.einsum('qhk,kd->qhd', weights.astype(jnp.bfloat16), value_block, pref...  17.4 us
    select_n x16, other arithmetic, turn(): return jax.tree.map(lambda a, b: jnp.where(reached, a, b), new, before)  14.9 us
    dot_general x8, matrix products, one_block(): jnp.einsum('qhd,kd->qhk', third_request_vector, key_block, preferred_elem...  9.77 us
  transfers between devices with their start and end apart: 3, of which 2 were waited for; matrix products, arithmetic and copies ran while one was open for 4% of the time, Pallas kernels for 0%

commit v1 on v0

--- a/solution.py
+++ b/solution.py
@@ -184,7 +184,9 @@
     )
     pieces = (
         lax.all_gather(key_mine, "ctx", axis=0, tiled=True),
-        lax.all_gather(value_mine, "ctx", axis=0, tiled=True),
+        jnp.concatenate(
+            lax.all_to_all(jnp.stack([value_mine] * lax.axis_size("ctx")), "ctx", 0, 0), axis=0
+        ),
     )
     start = jnp.int32(0)
     inner = tuple(

time: 477 us -> 445 us (0.933)
  waiting for transfers between devices: 90.7 us -> 22.1 us
  blocking collectives: 297 us -> 320 us
  starting transfers between devices: 0.12 us -> 14.1 us
    all_gather x1 -> x0, waiting for transfers between devices: 45.6 us -> none  [per_device(): lax.all_gather(value_mine, 'ctx', axis=0, tiled=True)]
    all_gather x1, waiting for transfers between devices: 45 us -> 22 us  [prefix(): lax.all_gather(part.astype(kind), axis)]
    all_to_all x0 -> x1, starting transfers between devices: none -> 14 us  [per_device(): lax.all_to_all(jnp.stack([value_mine] * lax.axis_size('ctx')), 'ctx', 0, 0)]
    psum x1, blocking collectives: 105 us -> 118 us  [per_device(): sums, counts = lax.psum((partial_sums, counted), ('ctx', 'head'))]
    unnamed x1, blocking collectives: 51.5 us -> 61.8 us
  transfers between devices with their start and end apart: 3 -> 3, of which waited for: 2 -> 1; matrix products, arithmetic and copies ran while one was open for 4% -> 5% of each run, Pallas kernels for 0% -> 0%
where the time goes in v1:
time: 445 us; the launch traced here: 443 us
  blocking collectives  320 us (72%)
  other arithmetic  32.3 us (7%)
  matrix products  26.5 us (6%)
  waiting for transfers between devices  22.1 us (5%)
  between operations  15.5 us (3%)
  starting transfers between devices  14.1 us (3%)
  local copies, waits for them, and re-layouts  12 us (3%)
    psum x1, blocking collectives, per_device(): squares = lax.psum(jnp.sum(gated * gated, axis=1), 'head')  141 us
    psum x1, blocking collectives, per_device(): sums, counts = lax.psum((partial_sums, counted), ('ctx', 'head'))  118 us
    unnamed x1, blocking collectives  61.8 us
    all_gather x1, waiting for transfers between devices, prefix(): lax.all_gather(part.astype(kind), axis)  22 us
    dot_general x8, matrix products, one_block(): jnp.einsum('qhk,kd->qhd', weights.astype(jnp.bfloat16), value_block, pref...  15.7 us
    select_n x16, other arithmetic, turn(): return jax.tree.map(lambda a, b: jnp.where(reached, a, b), new, before)  14.9 us
    all_to_all x1, starting transfers between devices, per_device(): lax.all_to_all(jnp.stack([value_mine] * lax.axis_size('ctx')), 'ctx', 0, 0)  14 us
    dot_general x8, matrix products, one_block(): jnp.einsum('qhd,kd->qhk', third_request_vector, key_block, preferred_elem...  9.78 us
  transfers between devices with their start and end apart: 3, of which 1 were waited for; matrix products, arithmetic and copies ran while one was open for 5% of the time, Pallas kernels for 0%

profile of v1, /device:TPU:1, one launch (start us, length us, event | category | flops | bytes accessed | tf_op | source)
XLA Modules:
  0.0 443.2 jit_solution(17581228373003950468)
XLA Ops:
  7.3 0.7 copy-done.12
  8.5 0.8 copy-done.2
  9.5 0.8 copy-done.3
  10.9 0.6 convert_element_type.90
  11.7 1.2 stack.2
  12.9 14.0 %all-to-all-start = ((bf16[16,256,128]{2,1,0:T(8,128)(2,1)}), bf16[16,256,128]{2,1,0:T(8,128)(2,1)S(1)}, u32[]{:S(2)}, u32[]{:S(2)}) async-start(bf16[16,256,128]{2,1,0:T(8,128)(2,1)} %stack.2), calls=%async_computation | async-start | bytes 2097152 | tf_op jit(solution)/shard_map/all_to_all | solution.py:188
  27.0 1.5 constant_dynamic-slice_fusion.1
  28.5 0.6 fusion.49
  30.0 1.3 dynamic-slice
  32.1 61.8 %all-reduce = bf16[32]{0:T(256)(128)(2,1)S(1)} all-reduce(bf16[32]{0:T(256)(128)(2,1)S(1)} %dynamic-update-slice), channel_id=2, replica_groups=mesh['ctx'=16,'head'=32] {'ctx'}, use_global_device_ids=true, to_apply=%add | all-reduce | flops 32 | bytes 128
  94.1 0.6 copy-done.11
  95.1 22.0 %all-gather.7.cloned.1.call-done = bf16[32,128,128]{2,1,0:T(8,128)(2,1)} async-done(((bf16[2,128,128]{2,1,0:T(8,128)(2,1)}), bf16[32,128,128]{2,1,0:T(8,128)(2,1)}) %all-gather.7.cloned.1.call-update) | async-done | bytes 1048592 | tf_op jit(solution)/shard_map/all_gather | solution.py:21
  117.1 15.6 %while.53 = (s32[]{:T(128)}, f32[2,128,128]{2,1,0:T(8,128)S(1)}, s32[]{:T(128)}, bf16[16,2]{1,0:T(8,128)(2,1)S(1)}, bf16[16,2,128,128]{3,2,1,0:T(8,128)(2,1)}) while((s32[]{:T(128)}, f32[2,128,128]{2,1,0:T(8,128)S(1)}, s32[]{:T(128)}, bf16[16,2]{1,0:T(8,128)(2,1)S(1)}, bf16[16,2,128,128]{3,2,1,0:T(8,128)(2,1)}) %tuple.137), condition=%wide.region_11.12_spmd.clone.clone, body=%wide.region_10.11_spmd.clone.sunk.clone | while | flops 163846 | bytes 327797 | solution.py:38
  117.1 0.9 fusion.84
  118.1 0.9 fusion.84
  119.1 0.9 fusion.84
  120.1 0.9 fusion.84
  121.0 0.9 fusion.84
  122.0 0.9 fusion.84
  123.0 0.9 fusion.84
  124.0 0.9 fusion.84
  124.9 0.9 fusion.84
  125.9 0.9 fusion.84
  126.9 0.9 fusion.84
  127.9 0.9 fusion.84
  128.8 0.9 fusion.84
  129.8 0.9 fusion.84
  130.8 0.9 fusion.84
  131.8 0.9 fusion.84
  132.7 0.6 copy-done.10
  134.0 0.7 copy-done.1
  134.8 140.6 %psum.21 = f32[256]{0:T(256)S(1)} all-reduce(f32[256]{0:T(256)S(1)} %multiply_reduce_fusion.2), channel_id=1, replica_groups=mesh['ctx'=16,'head'=32] {'head'}, use_global_device_ids=true, to_apply=%region_13.14 | all-reduce | flops 256 | bytes 2048 | tf_op jit(solution)/shard_map/psum | solution.py:165
  275.4 0.7 copy-done.7
  276.1 0.8 multiply_reduce_fusion
  277.0 38.6 %conditional.1 = (f32[256,2]{0,1:T(2,128)}, f32[256,2,128]{2,0,1:T(8,128)}) conditional(s32[]{:T(128)} %convert_element_type.82, () %tuple.48, (bf16[16,256,128]{2,1,0:T(8,128)(2,1)S(1)}, bf16[256,256]{1,0:T(8,128)(2,1)S(1)}, s32[256]{0:T(256)S(1)}, bf16[4096,128]{1,0:T(8,128)(2,1)}) %tuple.136), branch_computations={%region_1.2_spmd, %region_2.7_spmd} | conditional | flops 136907776 | bytes 5149947 | solution.py:80
  277.3 38.3 %while.51 = (s32[]{:T(128)}, f32[256,2]{0,1:T(2,128)S(1)}, f32[256,2]{0,1:T(2,128)}, f32[256,2,128]{2,0,1:T(8,128)}, s32[256]{0:T(256)S(1)}, /*index=5*/bf16[409...) while((s32[]{:T(128)}, f32[256,2]{0,1:T(2,128)S(1)}, ...), condition=%wide.region_6.6_spmd.clone.clone, body=%wide.region_3.5_spmd.clone.sunk.clone | while | flops 136907776 | bytes 4625571 | solution.py:74
  277.4 1.2 fusion.79
  278.9 0.6 fusion.82
  279.5 1.1 convolution_add_fusion.3
  280.8 1.2 fusion.79
  282.3 1.3 fusion.82
  283.6 2.1 convolution_add_fusion.3
  285.8 1.2 fusion.79
  287.3 1.3 fusion.82
  288.5 2.1 convolution_add_fusion.3
  290.8 1.2 fusion.79
  292.3 1.3 fusion.82
  293.5 2.1 convolution_add_fusion.3
  295.8 1.2 fusion.79
  297.3 1.3 fusion.82
  298.5 2.1 convolution_add_fusion.3
  300.8 1.2 fusion.79
  302.2 1.3 fusion.82
  303.5 2.1 convolution_add_fusion.3
  305.8 1.2 fusion.79
  307.2 1.3 fusion.82
  308.5 2.1 convolution_add_fusion.3
  310.8 1.2 fusion.79
  312.2 1.3 fusion.82
  313.5 2.1 convolution_add_fusion.3
  315.6 0.7 copy-done.9
  316.3 1.2 multiply_reduce_fusion.1
  317.6 0.7 copy_bitcast_fusion
  318.3 117.6 %all-reduce.1 = (f32[32]{0:T(128)S(1)}, f32[32]{0:T(128)S(1)}) all-reduce(f32[32]{0:T(128)S(1)} %convolution_bitcast_fusion.2, f32[32]{0:T(128)S(1)} %broadcast_multiply_fusion), channel_id=1, replica_groups=mesh['ctx'=16,'head'=32] {'ctx','head'}, use_global_device_ids=true, to_apply=%region_16.17 | all-reduce | flops 64 | bytes 512 | tf_op jit(solution)/shard_map/psum | solution.py:217
  (131 shorter events, 7.8 us)
Async XLA Ops:
  7.2 4.5 %copy-start = (bf16[256,1024]{1,0:T(8,128)(2,1)S(1)}, bf16[256,1024]{1,0:T(8,128)(2,1)}, u32[]{:S(2)}) copy-start(bf16[256,1024]{1,0:T(8,128)(2,1)} %param.24) | copy-start | bytes 1572868
  7.2 110.0 %all-gather.7.cloned.1.call-start = ((), (), s32[]{:S(2)}) async-start(), calls=%async_computation.2 | async-start | bytes 1114112 | tf_op jit(solution)/shard_map/all_gather | solution.py:21
  7.2 0.7 copy-start.12
  7.3 0.7 copy-start.6
  8.4 0.9 copy-start.2
  9.4 0.9 copy-start.3
  12.9 264.0 %all-to-all-start = ((bf16[16,256,128]{2,1,0:T(8,128)(2,1)}), bf16[16,256,128]{2,1,0:T(8,128)(2,1)S(1)}, u32[]{:S(2)}, u32[]{:S(2)}) async-start(bf16[16,256,128]{2,1,0:T(8,128)(2,1)} %stack.2), calls=%async_computation | async-start | bytes 2097152 | tf_op jit(solution)/shard_map/all_to_all | solution.py:188
  26.9 249.9 %all-gather.5.cloned.1.call-start = ((), (), s32[]{:S(2)}) async-start(), calls=%async_computation.1 | async-start | bytes 1114112 | tf_op jit(solution)/shard_map/all_gather | solution.py:186
  28.5 1.4 copy-start.4
  94.0 0.7 copy-start.11
  132.7 0.7 copy-start.10
  133.8 0.9 copy-start.1
  275.4 0.7 copy-start.7
  275.4 0.7 copy-start.8
  276.1 0.9 copy-start.5
  315.6 0.7 copy-start.9
Sparse Core Ops, SparseCore 0:
  11.7 105.3 all-gather.6
  119.8 99.0 all-gather.4
